TPU v7x, 256 devices: a whole 4x4x8 slice. The times are simulated.
256 devices in a mesh: row: 8 (over x_hi, y), col: 32 (over z, x_lo, core).
Axes of the slice: x: 4 (x_hi: 2, x_lo: 2; x = x_hi * 2 + x_lo), y: 4, z: 8, core: 2. Of those that a mesh axis runs over, the one named last changes fastest.
Arguments:
- pointmaps: bfloat16 [64, 64, 2, 3, 14336], P('row', 'col'), may hold values from -6 to 6
- confidence: bfloat16 [64, 64, 2, 14336], P('row', 'col'), may hold values from 1 to 10
- valid_blocks: int32 [64, 64, 64], P('row', 'col'), may hold values 0 or 1
- log_depth: float32 [64, 14336], P('row', 'col'), may hold values from 0 to 1.4
- camera: float32 [64, 8], replicated, may hold values from -1 to 5.8, as said below
- pair_pose: float32 [64, 64, 8], P('row', 'col'), may hold values from -1 to 1.2, as said below
- step_sizes: float32 [3], replicated, may hold values from 0.02 to 0.2
Outputs:
- new_log_depth: float32 [64, 14336], P('row', 'col')
- new_camera: float32 [64, 8], replicated
- new_pair_pose: float32 [64, 64, 8], P('row', 'col')
Inputs may be any that keep to these rules, and one draw needn't show every extreme that they name: `camera`: columns 0 to 3 hold a quaternion whose first entry lies in 0.8 to 1.2 and the others in -0.3 to 0.3; columns 4 to 6 a translation in -1 to 1; column 7 a log focal length in pixels, 5.2 to 5.8. `pair_pose`: columns 0 to 3 hold a quaternion whose first entry lies in 0.8 to 1.2 and the others in -0.3 to 0.3; columns 4 to 6 a translation in -1 to 1; column 7 a log scale in -0.5 to 0.5.
All inputs are finite; a program needn't handle non-finite values. No bound on the sum of `valid_blocks` on one device may be relied on, other than what follows from the above.
Results may differ from a plain program's by a relative error of at most 0.00055.
Values sent between devices are 32-bit elements; how exact they have to be, the bound alone decides.
A program may use at most 64 MiB of HBM per device.

v0:
```python
import jax
import jax.numpy as jnp
from jax import lax
from jax.sharding import PartitionSpec as P

IMAGES = 64
IMG_WIDTH = 224
IMG_HEIGHT = 224
WIN_ROWS = 64
ADAM_STEPS = 2


BETA_ONE = 0.9
BETA_TWO = 0.999
ADAM_EPS = 0.001
SOFTEN = 0.01


def from_root(value, axis, source):
    kept = jnp.where(lax.axis_index(axis) == source, value, 0).astype(value.dtype)
    return lax.psum(kept, axis)


def rotation(quaternion):
    length = jnp.sqrt(jnp.sum(quaternion * quaternion, axis=-1))
    w = quaternion[..., 0] / length
    x = quaternion[..., 1] / length
    y = quaternion[..., 2] / length
    z = quaternion[..., 3] / length
    return [
        [1.0 - 2.0 * (y * y + z * z), 2.0 * (x * y - w * z), 2.0 * (x * z + w * y)],
        [2.0 * (x * y + w * z), 1.0 - 2.0 * (x * x + z * z), 2.0 * (y * z - w * x)],
        [2.0 * (x * z - w * y), 2.0 * (y * z + w * x), 1.0 - 2.0 * (x * x + y * y)],
    ]


def world_points(log_depths, cameras):
    pixel_count = log_depths.shape[-1]
    position = jnp.arange(pixel_count, dtype=jnp.int32)
    across = (position % IMG_WIDTH).astype(jnp.float32) - (IMG_WIDTH - 1) / 2.0
    downward = (position // IMG_WIDTH + (IMG_HEIGHT - WIN_ROWS) // 2).astype(jnp.float32) - (
        IMG_HEIGHT - 1
    ) / 2.0
    focal_len = jnp.exp(cameras[:, 7:8])
    depth_map = jnp.exp(log_depths)
    ray_parts = (
        across[None, :] / focal_len * depth_map,
        downward[None, :] / focal_len * depth_map,
        depth_map,
    )
    turned = rotation(cameras[:, 0:4])
    return [
        turned[k][0][:, None] * ray_parts[0]
        + turned[k][1][:, None] * ray_parts[1]
        + turned[k][2][:, None] * ray_parts[2]
        + cameras[:, 4 + k][:, None]
        for k in range(3)
    ]


def pair_loss(
    first_depth,
    second_depth,
    first_camera,
    second_camera,
    pair_params,
    pointmaps,
    confidence,
    valid_blocks,
    first_ids,
    second_ids,
):
    first_world = world_points(first_depth, first_camera)
    second_world = world_points(second_depth, second_camera)
    pair_rotation = rotation(pair_params[..., 0:4])
    pair_scale = jnp.exp(pair_params[..., 7])
    pair_keep = (first_ids[:, None] != second_ids[None, :]).astype(jnp.float32)
    pixel_keep = (
        jnp.repeat(valid_blocks.astype(jnp.float32), IMG_WIDTH, axis=2) * pair_keep[:, :, None]
    )
    loss_sum = jnp.zeros((), jnp.float32)
    for side_index in range(2):
        if side_index == 0:
            points_side = [first_world[k][:, None, :] for k in range(3)]
        else:
            points_side = [second_world[k][None, :, :] for k in range(3)]
        source = [pointmaps[:, :, side_index, k, :].astype(jnp.float32) for k in range(3)]
        squared = SOFTEN
        for k in range(3):
            aligned = (
                pair_scale[..., None]
                * (
                    pair_rotation[k][0][..., None] * source[0]
                    + pair_rotation[k][1][..., None] * source[1]
                    + pair_rotation[k][2][..., None] * source[2]
                )
                + pair_params[..., 4 + k][..., None]
            )
            residual = points_side[k] - aligned
            squared = squared + residual * residual
        weight = confidence[:, :, side_index, :].astype(jnp.float32) * pixel_keep
        loss_sum = loss_sum + jnp.sum(weight * jnp.sqrt(squared))
    return loss_sum / (2.0 * (IMAGES - 1))


def adam_step(param, grad, first, second, step_number, step_size):
    first = BETA_ONE * first + (1.0 - BETA_ONE) * grad
    second = BETA_TWO * second + (1.0 - BETA_TWO) * grad * grad
    update = (
        step_size
        * (first / (1.0 - BETA_ONE**step_number))
        / (jnp.sqrt(second / (1.0 - BETA_TWO**step_number)) + ADAM_EPS)
    )
    return (param - update, first, second)


def body(pointmaps, confidence, valid_blocks, log_depth, camera, pair_pose, step_sizes):
    row_count = pointmaps.shape[0]
    col_count = pointmaps.shape[1]
    row_index = lax.axis_index("row")
    col_index = lax.axis_index("col")
    first_ids = row_index * row_count + jnp.arange(row_count, dtype=jnp.int32)
    second_ids = col_index * col_count + jnp.arange(col_count, dtype=jnp.int32)
    owner_row = col_index * col_count // row_count
    offset = col_index * col_count % row_count
    owner_flag = (row_index == owner_row).astype(jnp.float32)

    def local_loss(row_depth, col_depth, cameras, pair_params):
        first_camera = lax.dynamic_slice_in_dim(cameras, row_index * row_count, row_count, 0)
        second_camera = lax.dynamic_slice_in_dim(cameras, col_index * col_count, col_count, 0)
        return pair_loss(
            row_depth,
            col_depth,
            first_camera,
            second_camera,
            pair_params,
            pointmaps,
            confidence,
            valid_blocks,
            first_ids,
            second_ids,
        )

    depth_now, camera_now, pair_now = (log_depth, camera, pair_pose)
    depth_first = jnp.zeros_like(log_depth)
    depth_second = jnp.zeros_like(log_depth)
    camera_first = jnp.zeros_like(camera)
    camera_second = jnp.zeros_like(camera)
    pair_first = jnp.zeros_like(pair_pose)
    pair_second = jnp.zeros_like(pair_pose)
    for step_number in range(1, ADAM_STEPS + 1):
        row_depth = lax.all_gather(depth_now, "col", axis=1, tiled=True)
        picked = lax.dynamic_slice_in_dim(row_depth, offset, col_count, 0)
        col_depth = from_root(picked, "row", owner_row)
        row_grad, col_grad, cam_grad, pair_grad = jax.grad(local_loss, argnums=(0, 1, 2, 3))(
            row_depth, col_depth, camera_now, pair_now
        )
        col_total = lax.psum(col_grad, "row")
        placed = lax.dynamic_update_slice_in_dim(jnp.zeros_like(row_grad), col_total, offset, 0)
        rows_input = row_grad + owner_flag * placed
        depth_grad = lax.psum_scatter(rows_input, "col", scatter_dimension=1, tiled=True)
        cam_total = lax.psum(cam_grad, ("row", "col"))
        depth_now, depth_first, depth_second = adam_step(
            depth_now, depth_grad, depth_first, depth_second, step_number, step_sizes[0]
        )
        camera_now, camera_first, camera_second = adam_step(
            camera_now, cam_total, camera_first, camera_second, step_number, step_sizes[1]
        )
        pair_now, pair_first, pair_second = adam_step(
            pair_now, pair_grad, pair_first, pair_second, step_number, step_sizes[2]
        )
    return (depth_now, camera_now, pair_now)


def solution(mesh):
    in_specs = (
        P("row", "col", None, None, None),
        P("row", "col", None, None),
        P("row", "col", None),
        P("row", "col"),
        P(),
        P("row", "col", None),
        P(),
    )
    out_specs = (P("row", "col"), P(), P("row", "col", None))
    return jax.shard_map(body, mesh=mesh, in_specs=in_specs, out_specs=out_specs, check_vma=False)
```

profile of v0, /device:TPU:1, one launch (start us, length us, event | category | flops | bytes accessed | tf_op | source)
XLA Modules:
  0.0 819.1 jit_solution(6883007570498953672)
XLA Ops:
  7.2 40.2 %all-gather = f32[32,448,8]{1,2,0:T(8,128)S(1)} all-gather(f32[1,448,8]{1,2,0:T(8,128)} %bitcast.1591), channel_id=1, replica_groups=mesh['row'=8,'col'=32] {'col'}, dimensions={0}, use_global_device_ids=true | all-gather | bytes 473088 | tf_op jit(solution)/shard_map/all_gather | solution.py:152
  53.3 4.4 fusion.391
  57.7 5.4 fusion.390
  65.0 4.5 add_multiply_fusion.9
  70.3 5.0 multiply_reduce_fusion.8
  79.5 47.4 %all-reduce.65.cloned.1.call-done = f32[2,14336]{1,0:T(2,128)} async-done(((f32[2,14336]{1,0:T(2,128)}), f32[2,14336]{1,0:T(2,128)}) %all-reduce.65.cloned.1.call-update) | async-done | bytes 114704 | tf_op jit(solution)/shard_map/psum | solution.py:21
  128.3 4.9 add_multiply_fusion.8
  133.9 4.8 multiply_reduce_fusion.10
  138.8 3.0 multiply_reduce_fusion.36
  145.5 1.3 divide_subtract_fusion.2
  148.5 80.0 %all-reduce.67.cloned.1.call-done = f32[2,14336]{1,0:T(2,128)} async-done(((f32[2,14336]{1,0:T(2,128)}), f32[2,14336]{1,0:T(2,128)}) %all-reduce.67.cloned.1.call-update) | async-done | bytes 114704 | tf_op jit(solution)/shard_map/psum | solution.py:158
  229.5 3.4 fusion.90
  233.8 81.4 %psum.44 = f32[64,8]{0,1:T(8,128)S(1)} all-reduce(f32[64,8]{0,1:T(8,128)S(1)} %add_any.2128), channel_id=1, replica_groups=mesh['row'=8,'col'=32] {'row','col'}, use_global_device_ids=true, to_apply=%region_40.41 | all-reduce | flops 512 | bytes 4096 | tf_op jit(solution)/shard_map/psum | solution.py:162
  316.1 5.2 copy.99
  323.8 119.5 %reduce-scatter.7.cloned.1.call-done = f32[448,8]{1,0:T(8,128)} async-done(((f32[14336,8]{1,0:T(8,128)}), f32[448,8]{1,0:T(8,128)}) %reduce-scatter.7.cloned.1.call-update) | async-done | bytes 14352
  444.8 35.6 %all-gather.1 = f32[32,448,8]{1,2,0:T(8,128)S(1)} all-gather(f32[1,448,8]{1,2,0:T(8,128)S(1)} %fusion.385), channel_id=1, replica_groups=mesh['row'=8,'col'=32] {'col'}, dimensions={0}, use_global_device_ids=true | all-gather | bytes 473088 | tf_op jit(solution)/shard_map/all_gather | solution.py:152
  481.5 2.1 reshape.1655
  483.6 1.7 select_bitcast_fusion
  485.3 1.5 fusion.67
  486.9 3.8 add_multiply_fusion.3
  490.7 2.0 add_multiply_fusion.4
  492.8 6.5 multiply_reduce_fusion.2
  501.0 71.3 %all-reduce.69.cloned.1.call-done = f32[2,14336]{1,0:T(2,128)} async-done(((f32[2,14336]{1,0:T(2,128)}), f32[2,14336]{1,0:T(2,128)}) %all-reduce.69.cloned.1.call-update) | async-done | bytes 114704 | tf_op jit(solution)/shard_map/psum | solution.py:21
  572.3 1.4 add_add_fusion
  573.8 2.7 add_multiply_fusion
  577.3 4.6 multiply_reduce_fusion.4
  582.0 1.9 multiply_reduce_fusion.25
  590.1 80.5 %all-reduce.71.cloned.1.call-done = f32[2,14336]{1,0:T(2,128)} async-done(((f32[2,14336]{1,0:T(2,128)}), f32[2,14336]{1,0:T(2,128)}) %all-reduce.71.cloned.1.call-update) | async-done | bytes 114704 | tf_op jit(solution)/shard_map/psum | solution.py:158
  671.6 2.2 fusion.74
  673.9 4.8 copy.101
  679.1 82.1 %psum.47 = f32[64,8]{0,1:T(8,128)S(1)} all-reduce(f32[64,8]{0,1:T(8,128)S(1)} %add_any.2401), channel_id=1, replica_groups=mesh['row'=8,'col'=32] {'row','col'}, use_global_device_ids=true, to_apply=%region_111.112 | all-reduce | flops 512 | bytes 4096 | tf_op jit(solution)/shard_map/psum | solution.py:162
  761.7 47.8 %reduce-scatter.9.cloned.1.call-done = f32[448,8]{1,0:T(8,128)} async-done(((f32[14336,8]{1,0:T(8,128)}), f32[448,8]{1,0:T(8,128)}) %reduce-scatter.9.cloned.1.call-update) | async-done | bytes 14352
  (191 shorter events, 38.8 us)
Async XLA Ops:
  7.2 119.7 %all-reduce.65.cloned.1.call-start = ((), (), s32[]{:S(2)}) async-start(), calls=%async_computation.2 | async-start | bytes 229376 | tf_op jit(solution)/shard_map/psum | solution.py:21
  47.9 16.6 %copy-start.4 = (f32[14336,8]{0,1:T(8,128)}, f32[14336,8]{0,1:T(8,128)S(1)}, u32[]{:S(2)}) copy-start(f32[14336,8]{0,1:T(8,128)S(1)} %reshape.1653) | copy-start | bytes 1376260
  48.8 179.7 %all-reduce.67.cloned.1.call-start = ((), (), s32[]{:S(2)}) async-start(), calls=%async_computation.3 | async-start | bytes 229376 | tf_op jit(solution)/shard_map/psum | solution.py:158
  53.3 9.9 %copy-start.11 = (f32[64,8]{0,1:T(8,128)S(1)}, f32[64,8]{0,1:T(8,128)}, u32[]{:S(2)}) copy-start(f32[64,8]{0,1:T(8,128)} %param.11) | copy-start | bytes 6148
  53.3 10.0 %copy-start.12 = (f32[3]{0:T(128)S(1)}, f32[3]{0:T(128)}, u32[]{:S(2)}) copy-start(f32[3]{0:T(128)} %param.13) | copy-start | bytes 40
  57.7 11.8 %copy-start.3 = (bf16[8,2,1,14336]{3,2,1,0:T(2,128)(2,1)}, bf16[8,2,1,14336]{3,2,1,0:T(2,128)(2,1)S(1)}, u32[]{:S(2)}) copy-start(bf16[8,2,1,14336]{3,2,1,0:T(2,128)(2,1)S(1)} %get-tuple-element.220) | copy-start | bytes 1376260
  78.9 49.3 %copy-start.29 = (f32[2]{0:T(128)}, f32[2]{0:T(128)S(1)}, u32[]{:S(2)}) copy-start(f32[2]{0:T(128)S(1)} %get-tuple-element.348) | copy-start | bytes 28
  78.9 59.8 %copy-start.27 = (f32[2]{0:T(128)}, f32[2]{0:T(128)S(1)}, u32[]{:S(2)}) copy-start(f32[2]{0:T(128)S(1)} %get-tuple-element.337) | copy-start | bytes 28
  78.9 59.8 %copy-start.28 = (f32[2]{0:T(128)}, f32[2]{0:T(128)S(1)}, u32[]{:S(2)}) copy-start(f32[2]{0:T(128)S(1)} %get-tuple-element.347) | copy-start | bytes 28
  128.2 10.5 %copy-start.8 = (f32[2,14336]{1,0:T(2,128)S(1)}, f32[2,14336]{1,0:T(2,128)}, u32[]{:S(2)}) copy-start(f32[2,14336]{1,0:T(2,128)} %all-reduce.65.cloned.1.call-done) | copy-start | bytes 344068
  128.3 10.5 %copy-start.30 = (f32[2]{0:T(128)S(1)}, f32[2]{0:T(128)}, u32[]{:S(2)}) copy-start(f32[2]{0:T(128)} %copy-done.29) | copy-start | bytes 28
  128.3 10.5 %copy-start.32 = (f32[2]{0:T(128)S(1)}, f32[2]{0:T(128)}, u32[]{:S(2)}) copy-start(f32[2]{0:T(128)} %get-tuple-element.309) | copy-start | bytes 28
  141.9 301.3 %reduce-scatter.7.cloned.1.call-start = ((), (), s32[]{:S(2)}) async-start(), calls=%async_computation.6 | async-start | bytes 7569408
  316.1 128.2 %copy-start.10 = (f32[8,448]{1,0:T(8,128)S(1)}, f32[8,448]{1,0:T(8,128)}, u32[]{:S(2)}) copy-start(f32[8,448]{1,0:T(8,128)} %param.10) | copy-start | bytes 43012
  321.4 250.9 %all-reduce.69.cloned.1.call-start = ((), (), s32[]{:S(2)}) async-start(), calls=%async_computation.4 | async-start | bytes 229376 | tf_op jit(solution)/shard_map/psum | solution.py:21
  323.2 169.5 %copy-start.13 = (f32[2,1]{0,1:T(1,128)}, f32[2,1]{0,1:T(1,128)S(1)}, u32[]{:S(2)}) copy-start(f32[2,1]{0,1:T(1,128)S(1)} %get-tuple-element.287) | copy-start | bytes 28
  323.2 169.5 %copy-start.15 = (f32[2,1]{0,1:T(1,128)}, f32[2,1]{0,1:T(1,128)S(1)}, u32[]{:S(2)}) copy-start(f32[2,1]{0,1:T(1,128)S(1)} %get-tuple-element.288) | copy-start | bytes 28
  492.7 177.9 %all-reduce.71.cloned.1.call-start = ((), (), s32[]{:S(2)}) async-start(), calls=%async_computation.5 | async-start | bytes 229376 | tf_op jit(solution)/shard_map/psum | solution.py:158
  572.3 9.7 %copy-start.20 = (f32[2]{0:T(128)S(1)}, f32[2]{0:T(128)}, u32[]{:S(2)}) copy-start(f32[2]{0:T(128)} %get-tuple-element.320) | copy-start | bytes 28
  572.3 9.7 %copy-start.21 = (f32[2]{0:T(128)S(1)}, f32[2]{0:T(128)}, u32[]{:S(2)}) copy-start(f32[2]{0:T(128)} %get-tuple-element.321) | copy-start | bytes 28
  572.3 9.7 %copy-start.22 = (f32[2]{0:T(128)S(1)}, f32[2]{0:T(128)}, u32[]{:S(2)}) copy-start(f32[2]{0:T(128)} %get-tuple-element.322) | copy-start | bytes 28
  572.3 9.7 %copy-start.23 = (f32[2]{0:T(128)S(1)}, f32[2]{0:T(128)}, u32[]{:S(2)}) copy-start(f32[2]{0:T(128)} %get-tuple-element.323) | copy-start | bytes 28
  572.3 9.7 %copy-start.24 = (f32[2]{0:T(128)S(1)}, f32[2]{0:T(128)}, u32[]{:S(2)}) copy-start(f32[2]{0:T(128)} %get-tuple-element.324) | copy-start | bytes 28
  572.3 9.7 %copy-start.25 = (f32[2]{0:T(128)S(1)}, f32[2]{0:T(128)}, u32[]{:S(2)}) copy-start(f32[2]{0:T(128)} %get-tuple-element.343) | copy-start | bytes 28
  572.3 9.7 %copy-start.26 = (f32[2]{0:T(128)S(1)}, f32[2]{0:T(128)}, u32[]{:S(2)}) copy-start(f32[2]{0:T(128)} %get-tuple-element.344) | copy-start | bytes 28
  572.3 9.7 %copy-start.31 = (f32[2]{0:T(128)S(1)}, f32[2]{0:T(128)}, u32[]{:S(2)}) copy-start(f32[2]{0:T(128)} %get-tuple-element.281) | copy-start | bytes 28
  573.7 10.2 %copy-start.14 = (f32[2,1]{0,1:T(1,128)S(1)}, f32[2,1]{0,1:T(1,128)}, u32[]{:S(2)}) copy-start(f32[2,1]{0,1:T(1,128)} %copy-done.13) | copy-start | bytes 28
  573.7 10.2 %copy-start.16 = (f32[2,1]{0,1:T(1,128)S(1)}, f32[2,1]{0,1:T(1,128)}, u32[]{:S(2)}) copy-start(f32[2,1]{0,1:T(1,128)} %copy-done.15) | copy-start | bytes 28
  573.7 97.9 %copy-start.5 = (f32[14336,8]{0,1:T(8,128)S(1)}, f32[14336,8]{0,1:T(8,128)}, u32[]{:S(2)}) copy-start(f32[14336,8]{0,1:T(8,128)} %reshape.1655) | copy-start | bytes 1376260
  576.5 95.1 %copy-start.6 = (f32[8,14336]{1,0:T(8,128)S(1)}, f32[8,14336]{1,0:T(8,128)}, u32[]{:S(2)}) copy-start(f32[8,14336]{1,0:T(8,128)} %get-tuple-element.90) | copy-start | bytes 1376260
  576.5 95.1 %copy-start.7 = (f32[8,14336]{1,0:T(8,128)S(1)}, f32[8,14336]{1,0:T(8,128)}, u32[]{:S(2)}) copy-start(f32[8,14336]{1,0:T(8,128)} %get-tuple-element.93) | copy-start | bytes 1376260
  584.0 225.5 %reduce-scatter.9.cloned.1.call-start = ((), (), s32[]{:S(2)}) async-start(), calls=%async_computation.7 | async-start | bytes 7569408
  (10 other events, 64.1 us)
Sparse Core Ops, SparseCore 0:
  48.9 77.9 all-reduce.64
  142.0 86.4 all-reduce.66
  321.5 121.7 reduce-scatter.6
  492.9 79.3 all-reduce.68
  584.1 86.4 all-reduce.70
  678.8 130.6 reduce-scatter.8
where the time goes:
time: 826 us; the launch traced here: 819 us
  waiting for transfers between devices  447 us (54%)
  blocking collectives  239 us (29%)
  other arithmetic  82.2 us (10%)
  local copies, waits for them, and re-layouts  33.6 us (4%)
  between operations  17.1 us (2%)
    unnamed x8, waiting for transfers between devices  167 us
    psum x2, blocking collectives, body(): cam_total = lax.psum(cam_grad, ('row', 'col'))  164 us
    psum x2, waiting for transfers between devices, body(): col_total = lax.psum(col_grad, 'row')  161 us
    psum x2, waiting for transfers between devices, from_root(): return lax.psum(kept, axis)  119 us
    all_gather x2, blocking collectives, body(): row_depth = lax.all_gather(depth_now, 'col', axis=1, tiled=True)  75.8 us
    reduce_sum x4, other arithmetic, pair_loss(): pair_scale[..., None]  21 us
    add_any x8, other arithmetic, pair_loss(): squared = squared + residual * residual  20.3 us
  transfers between devices with their start and end apart: 6, of which 6 were waited for; matrix products, arithmetic and copies ran while one was open for 6% of the time, Pallas kernels for 0%

commit v1 on v0

v1 whole, which is shorter than its diff:
```python
import jax
import jax.numpy as jnp
from jax import lax
from jax.experimental import pallas as pl
from jax.experimental.pallas import tpu as pltpu
from jax.sharding import PartitionSpec as P

IMAGES = 64
IMG_WIDTH = 224
IMG_HEIGHT = 224
WIN_ROWS = 64
ADAM_STEPS = 2
BETA_ONE = 0.9
BETA_TWO = 0.999
ADAM_EPS = 0.001
SOFTEN = 0.01

ROWS = 8
COLS = 32
CHIPS = COLS // 2
HALF = 448
WIDE = 512
TILES = 7
STRIP = 896
LANES = 128
MESH = pl.DeviceIdType.MESH
F32 = jnp.float32


def rotation(quaternion):
    length = jnp.sqrt(sum(value * value for value in quaternion))
    w, x, y, z = [value / length for value in quaternion]
    turned = [
        [1.0 - 2.0 * (y * y + z * z), 2.0 * (x * y - w * z), 2.0 * (x * z + w * y)],
        [2.0 * (x * y + w * z), 1.0 - 2.0 * (x * x + z * z), 2.0 * (y * z - w * x)],
        [2.0 * (x * z - w * y), 2.0 * (y * z + w * x), 1.0 - 2.0 * (x * x + y * y)],
    ]
    return turned, (w, x, y, z), length


def rotation_grad(h, unit, length):
    w, x, y, z = unit
    dw = 2.0 * (z * (h[1][0] - h[0][1]) + y * (h[0][2] - h[2][0]) + x * (h[2][1] - h[1][2]))
    dx = 2.0 * (
        y * (h[0][1] + h[1][0]) + z * (h[0][2] + h[2][0]) + w * (h[2][1] - h[1][2]) - 2.0 * x * (h[1][1] + h[2][2])
    )
    dy = 2.0 * (
        x * (h[0][1] + h[1][0]) + z * (h[1][2] + h[2][1]) + w * (h[0][2] - h[2][0]) - 2.0 * y * (h[0][0] + h[2][2])
    )
    dz = 2.0 * (
        x * (h[0][2] + h[2][0]) + y * (h[1][2] + h[2][1]) + w * (h[1][0] - h[0][1]) - 2.0 * z * (h[0][0] + h[1][1])
    )
    along = w * dw + x * dx + y * dy + z * dz
    return [(dw - w * along) / length, (dx - x * along) / length, (dy - y * along) / length, (dz - z * along) / length]


def adam_step(param, grad, first, second, fix_one, fix_two, step_size):
    first = BETA_ONE * first + (1.0 - BETA_ONE) * grad
    second = BETA_TWO * second + (1.0 - BETA_TWO) * grad * grad
    update = step_size * (first / fix_one) / (jnp.sqrt(second / fix_two) + ADAM_EPS)
    return param - update, first, second


def lane_sum(value):
    return jnp.broadcast_to(jnp.sum(value, axis=1, keepdims=True), (8, LANES))


def full_sum(value):
    return jnp.broadcast_to(jnp.sum(jnp.sum(value, axis=0, keepdims=True), axis=1, keepdims=True), (8, LANES))


def kernel(
    maps_hbm, conf_hbm, valid_ref, depth_in, camera_in, pair_in, rates,
    depth_out, camera_out, pair_out,
    raw, raw_conf, planes, uv, coef, tmp, acc_pair, acc_row, acc_col,
    depth, depth_m, depth_v, pose, pose_m, pose_v, cam, cam_m, cam_v,
    row_depth, all_depth, col_depth,
    row_grad, row_sib, row_sum, row_recv, col_grad, col_recv, col_owner,
    cam_sib, cam_row, cam_all,
    load_sem, send_sem, recv_sem,
):
    r = lax.axis_index("row")
    c = lax.axis_index("col")
    q = lax.rem(c, 2)
    g = lax.div(c, 2)
    z = lax.div(c, 4)
    sibling = {"col": 2 * g + 1 - q}
    lane = lax.broadcasted_iota(jnp.int32, (8, LANES), 1)
    sub = lax.broadcasted_iota(jnp.int32, (8, LANES), 0)
    low = lane < 64

    def chip_at(n):
        half = lax.div(n + 1, 2)
        return lax.rem(g + 8 + half * (1 - 2 * lax.rem(n, 2)), CHIPS)

    def row_at(n):
        return lax.rem(r + 1 + n, ROWS)

    def remote(src, dst, kind, st, device):
        return pltpu.make_async_remote_copy(
            src_ref=src, dst_ref=dst, send_sem=send_sem.at[kind], recv_sem=recv_sem.at[kind, st],
            device_id=device, device_id_type=MESH,
        )

    def wait_bytes(ref, sem):
        pltpu.make_async_copy(ref, ref, sem).wait()

    def to_chips(make):
        def one(n, carry):
            make(chip_at(n)).start()
            return carry
        lax.fori_loop(0, CHIPS - 1, one, 0)

    def to_rows(make):
        def one(n, carry):
            make(row_at(n)).start()
            return carry
        lax.fori_loop(0, ROWS - 1, one, 0)

    load_maps = pltpu.make_async_copy(maps_hbm, raw, load_sem.at[0])
    load_conf = pltpu.make_async_copy(conf_hbm, raw_conf, load_sem.at[1])
    load_maps.start()
    load_conf.start()

    barrier = pltpu.get_barrier_semaphore()

    def greet_chip(n, carry):
        pl.semaphore_signal(barrier, inc=1, device_id={"col": 2 * chip_at(n) + q}, device_id_type=MESH)
        return carry

    def greet_row(n, carry):
        pl.semaphore_signal(barrier, inc=1, device_id={"row": row_at(n)}, device_id_type=MESH)
        return carry

    lax.fori_loop(0, CHIPS - 1, greet_chip, 0)
    lax.fori_loop(0, ROWS - 1, greet_row, 0)
    pl.semaphore_signal(barrier, inc=1, device_id=sibling, device_id_type=MESH)

    depth[...] = jnp.zeros_like(depth)
    depth[:, 0:HALF] = depth_in[...]
    for ref in (depth_m, depth_v, pose_m, pose_v, cam_m, cam_v):
        ref[...] = jnp.zeros_like(ref)
    for j in range(2):
        loaded = pair_in[:, j, :]
        for k in range(8):
            pose[j, k] = jnp.broadcast_to(loaded[:, k : k + 1], (8, LANES))
    cam[...] = jnp.zeros_like(cam)
    cam[:, 0:IMAGES] = camera_in[...]
    for t in range(TILES):
        position = lane + t * LANES
        downward = (
            (position >= IMG_WIDTH).astype(jnp.int32)
            + (position >= 2 * IMG_WIDTH).astype(jnp.int32)
            + (position >= 3 * IMG_WIDTH).astype(jnp.int32)
        )
        uv[t, 0] = (position - IMG_WIDTH * downward).astype(F32) - (IMG_WIDTH - 1) / 2.0
        uv[t, 1] = downward.astype(F32) + ((IMG_HEIGHT - WIN_ROWS) // 2 - (IMG_HEIGHT - 1) / 2.0)

    pl.semaphore_wait(barrier, CHIPS - 1 + ROWS - 1 + 1)

    def plane_base(j, tile, s):
        return ((j * 112 + tile) * 2 + s) * 32

    def prepare(m, carry):
        for j in range(2):
            here = valid_ref[:, j, :].astype(F32)
            lane64 = lax.broadcasted_iota(jnp.int32, (8, WIN_ROWS), 1)
            other = (ROWS * r + sub) != (2 * c + j)
            scale = jnp.where(other, 1.0 / (2.0 * (IMAGES - 1)), 0.0)
            line = [
                scale * jnp.broadcast_to(
                    jnp.sum(jnp.where(lane64 == 4 * m + a, here, 0.0), axis=1, keepdims=True), (8, LANES))
                for a in range(4)
            ]
            for t in range(TILES):
                start = pl.multiple_of(m * STRIP + t * LANES, LANES)
                tile = m * TILES + t
                base = pl.multiple_of(plane_base(j, tile, 0), 64)
                for i in range(8):
                    for k in range(3):
                        planes[pl.ds(base + 8 * k + i, 2, stride=32), :] = raw[
                            i, j, k, :, pl.ds(start, LANES)].astype(F32)
                    planes[pl.ds(base + 24 + i, 2, stride=32), :] = raw_conf[
                        i, j, :, pl.ds(start, LANES)].astype(F32)
                first = t * LANES // IMG_WIDTH
                split = (first + 1) * IMG_WIDTH - t * LANES
                keep = line[first] if split >= LANES else jnp.where(lane < split, line[first], line[first + 1])
                for s in range(2):
                    at = pl.ds(pl.multiple_of(base + 32 * s + 24, 8), 8)
                    planes[at, :] = planes[at, :] * keep
        return carry

    def camera_of_rows():
        now = cam[...]
        mine = lane == 8 * r + sub
        return [lane_sum(jnp.where(mine, jnp.broadcast_to(now[k : k + 1, :], (8, LANES)), 0.0)) for k in range(8)]

    def camera_of_col(j):
        now = cam[...]
        mine = lane == 2 * c + j
        return [full_sum(jnp.where(mine & (sub == k), now, 0.0)) for k in range(8)]

    def element(base, at, z3, total):
        x = [planes[pl.ds(pl.multiple_of(base + 8 * k, 8), 8), :] for k in range(3)]
        weight = planes[pl.ds(pl.multiple_of(base + 24, 8), 8), :]
        residual = [
            z3[k] - (at[9 + k] + at[3 * k] * x[0] + at[3 * k + 1] * x[1] + at[3 * k + 2] * x[2]) for k in range(3)
        ]
        squared = SOFTEN + residual[0] * residual[0] + residual[1] * residual[1] + residual[2] * residual[2]
        pull = weight * lax.rsqrt(squared)
        grads = [pull * residual[k] for k in range(3)]
        terms = [grads[k] * x[n] for k in range(3) for n in range(3)] + grads
        total = terms if total is None else [a + b for a, b in zip(total, terms)]
        return grads, total

    def moments(grads, value, u, v, total):
        h = [grads[k] * value for k in range(3)]
        terms = [h[k] * u for k in range(3)] + [h[k] * v for k in range(3)] + h + list(grads)
        return terms if total is None else [a + b for a, b in zip(total, terms)]

    def rays(first, t, down):
        u = uv[t, 0]
        v = uv[t, 1] + down
        return u, v, [coef[first + k] * u + (coef[first + 3 + k] * v + coef[first + 6 + k]) for k in range(3)]

    def pair_at(j, s):
        first = 27 + 15 * j
        return [coef[first + k] for k in range(9)] + [coef[first + 9 + 3 * s + k] for k in range(3)]

    def strip_tiles(left, right):
        rolled = pltpu.roll(right, 64, 1)
        middle = jnp.where(low[0 : left.shape[0]], left[:, 384:512], rolled[:, 0:128])
        return [left[:, 0:128], left[:, 128:256], left[:, 256:384], middle,
                rolled[:, 128:256], rolled[:, 256:384], rolled[:, 384:512]]

    def side_rows(st):
        def body(m, carry):
            tiles = strip_tiles(row_depth[st, 0, m], row_depth[st, 1, m])
            down = (4 * m).astype(F32)
            for t in range(TILES):
                value = jnp.exp(tiles[t])
                u, v, ray = rays(0, t, down)
                tmp[t, 6] = value
                for k in range(3):
                    tmp[t, k] = value * ray[k]
            for j in range(2):
                at = pair_at(j, 0)
                total = None
                for t in range(TILES):
                    z3 = [tmp[t, k] for k in range(3)]
                    grads, total = element(plane_base(j, m * TILES + t, 0), at, z3, total)
                    for k in range(3):
                        tmp[t, 3 + k] = grads[k] if j == 0 else tmp[t, 3 + k] + grads[k]
                for k in range(12):
                    acc_pair[j, k] += total[k]
            total = None
            out = []
            for t in range(TILES):
                grads = [tmp[t, 3 + k] for k in range(3)]
                z3 = [tmp[t, k] for k in range(3)]
                out.append(grads[0] * z3[0] + grads[1] * z3[1] + grads[2] * z3[2])
                total = moments(grads, tmp[t, 6], uv[t, 0], uv[t, 1] + down, total)
            for k in range(12):
                acc_row[k] += total[k]
            row_grad[0, m] = jnp.concatenate(out[0:4], axis=1)
            row_grad[1, m] = pltpu.roll(jnp.concatenate(out[3:7], axis=1), 448, 1)
            return carry
        return body

    def side_cols(st):
        def body(m, carry):
            tiles = strip_tiles(col_depth[st, 0, m, q], col_depth[st, 1, m, q])
            values = [jnp.exp(tile) for tile in tiles]
            down = (4 * m).astype(F32)
            for j in range(2):
                at = pair_at(j, 1)
                total = None
                cam_total = None
                out = []
                for t in range(TILES):
                    value = jnp.broadcast_to(values[t][j : j + 1, :], (8, LANES))
                    u, v, ray = rays(9 + 9 * j, t, down)
                    z3 = [value * ray[k] for k in range(3)]
                    grads, total = element(plane_base(j, m * TILES + t, 1), at, z3, total)
                    mine = grads[0] * z3[0] + grads[1] * z3[1] + grads[2] * z3[2]
                    out.append(jnp.sum(mine, axis=0, keepdims=True))
                    cam_total = moments(grads, value, u, v, cam_total)
                for k in range(12):
                    acc_pair[j, k] += total[k]
                for k in range(12):
                    acc_col[j, k] += cam_total[k]
                col_grad[st, 0, m, q, j : j + 1, :] = jnp.concatenate(out[0:4], axis=1)
                col_grad[st, 1, m, q, j : j + 1, :] = pltpu.roll(jnp.concatenate(out[3:7], axis=1), 448, 1)
            return carry
        return body

    def camera_grad(values, total):
        turned, unit, length = rotation(values[0:4])
        inverse = jnp.exp(-values[7])
        h = [[total[k] * inverse, total[3 + k] * inverse, total[6 + k]] for k in range(3)]
        focal = sum(turned[k][0] * h[k][0] + turned[k][1] * h[k][1] for k in range(3))
        return rotation_grad(h, unit, length) + [total[9], total[10], total[11], -focal]

    ROW_ALL, ROW_FWD, OWN_COL, COL_ALL, COL_FWD, GR_SIB, GR_ALL, GC_SIB, GC_ALL, GC_OWN, CA_SIB, CA_ROW, CA_ALL = range(13)

    def step(st, carry):
        late = (st > 0).astype(F32)
        fix_one = (1.0 - BETA_ONE) + late * ((1.0 - BETA_ONE**2) - (1.0 - BETA_ONE))
        fix_two = (1.0 - BETA_TWO) + late * ((1.0 - BETA_TWO**2) - (1.0 - BETA_TWO))

        now = depth[...]
        for x in range(2):
            for k in range(2):
                all_depth[st, r, x, k] = now[4 * x + 2 * k : 4 * x + 2 * k + 2, :]
        row_depth[st, q, g] = now
        to_rows(lambda p: remote(all_depth.at[st, r], all_depth.at[st, r], OWN_COL, st, {"row": p}))
        to_chips(lambda p: remote(row_depth.at[st, q, g], row_depth.at[st, q, g], ROW_ALL, st, {"col": 2 * p + q}))

        @pl.when(st == 0)
        def _():
            load_maps.wait()
            load_conf.wait()
            lax.fori_loop(0, CHIPS // 2, prepare, 0)

        @pl.when(st > 0)
        def _():
            wait_bytes(cam_all.at[st - 1, pl.ds(0, ROWS - 1)], recv_sem.at[CA_ALL, st - 1])
            grad = cam_all[st - 1, 0]
            for p in range(1, ROWS):
                grad = grad + cam_all[st - 1, p]
            cam[...], cam_m[...], cam_v[...] = adam_step(
                cam[...], grad, cam_m[...], cam_v[...], 1.0 - BETA_ONE, 1.0 - BETA_TWO, rates[1])

        wait_bytes(all_depth.at[st, pl.ds(0, ROWS - 1)], recv_sem.at[OWN_COL, st])
        col_depth[st, q, g] = all_depth[st, z, lax.rem(g, 2)]
        to_chips(lambda p: remote(
            all_depth.at[st, lax.div(p, 2), lax.rem(p, 2)], col_depth.at[st, q, g], COL_ALL, st, {"col": 2 * p + q}))

        wait_bytes(row_depth.at[st, q, pl.ds(0, CHIPS - 1)], recv_sem.at[ROW_ALL, st])
        row_fwd = remote(row_depth.at[st, q], row_depth.at[st, q], ROW_FWD, st, sibling)
        row_fwd.start()

        @pl.when(st == 0)
        def _():
            lax.fori_loop(CHIPS // 2, CHIPS, prepare, 0)

        values = camera_of_rows()
        turned, _, _ = rotation(values[0:4])
        inverse = jnp.exp(-values[7])
        shift = [[None] * 2, [None] * 2]
        for k in range(3):
            coef[k] = turned[k][0] * inverse
            coef[3 + k] = turned[k][1] * inverse
            coef[6 + k] = turned[k][2]
        shift[0][0] = shift[0][1] = values[4:7]
        for j in range(2):
            values = camera_of_col(j)
            turned, _, _ = rotation(values[0:4])
            inverse = jnp.exp(-values[7])
            for k in range(3):
                coef[9 + 9 * j + k] = turned[k][0] * inverse
                coef[9 + 9 * j + 3 + k] = turned[k][1] * inverse
                coef[9 + 9 * j + 6 + k] = turned[k][2]
            shift[1][j] = values[4:7]
        for j in range(2):
            values = [pose[j, k] for k in range(8)]
            turned, _, _ = rotation(values[0:4])
            scale = jnp.exp(values[7])
            first = 27 + 15 * j
            for k in range(3):
                for n in range(3):
                    coef[first + 3 * k + n] = scale * turned[k][n]
                for s in range(2):
                    coef[first + 9 + 3 * s + k] = values[4 + k] - shift[s][j][k]
        for ref in (acc_pair, acc_row, acc_col):
            ref[...] = jnp.zeros_like(ref)

        wait_bytes(row_depth.at[st, 1 - q], recv_sem.at[ROW_FWD, st])
        lax.fori_loop(0, CHIPS // 2, side_rows(st), 0)
        wait_bytes(col_depth.at[st, q, pl.ds(0, CHIPS - 1)], recv_sem.at[COL_ALL, st])
        col_fwd = remote(col_depth.at[st, q, :, 1 - q], col_depth.at[st, q, :, 1 - q], COL_FWD, st, sibling)
        col_fwd.start()
        lax.fori_loop(CHIPS // 2, CHIPS, side_rows(st), 0)

        row_swap = remote(row_grad.at[1 - q], row_sib.at[st], GR_SIB, st, sibling)
        row_swap.start()
        wait_bytes(col_depth.at[st, 1 - q, :, q], recv_sem.at[COL_FWD, st])
        lax.fori_loop(0, CHIPS // 2, side_cols(st), 0)
        wait_bytes(row_sib.at[st], recv_sem.at[GR_SIB, st])

        def add_sibling(m, carry):
            row_sum[m] = row_grad[q, m] + row_sib[st, m]
            return carry

        lax.fori_loop(0, CHIPS, add_sibling, 0)
        row_recv[st, g] = row_sum[g]
        to_chips(lambda p: remote(row_sum.at[p], row_recv.at[st, g], GR_ALL, st, {"col": 2 * p + q}))
        lax.fori_loop(CHIPS // 2, CHIPS, side_cols(st), 0)

        col_swap = remote(col_grad.at[st, 1 - q, :, q], col_grad.at[st, 1 - q, :, q], GC_SIB, st, sibling)
        col_swap.start()

        values = camera_of_rows()
        part = camera_grad(values, [lane_sum(acc_row[k]) for k in range(12)])
        rows = [jnp.where(lane == 8 * r + sub, part[k], 0.0) for k in range(8)]
        mine = jnp.concatenate([jnp.sum(row, axis=0, keepdims=True) for row in rows], axis=0)
        for j in range(2):
            values = camera_of_col(j)
            part = camera_grad(values, [full_sum(acc_col[j, k]) for k in range(12)])
            for k in range(8):
                mine = mine + jnp.where((sub == k) & (lane == 2 * c + j), part[k], 0.0)
        cam_sib[st, q] = mine
        cam_swap = remote(cam_sib.at[st, q], cam_sib.at[st, q], CA_SIB, st, sibling)
        cam_swap.start()

        wait_bytes(col_grad.at[st, q, :, 1 - q], recv_sem.at[GC_SIB, st])
        col_recv[st, g] = col_grad[st, q, g]
        to_chips(lambda p: remote(col_grad.at[st, q, p], col_recv.at[st, g], GC_ALL, st, {"col": 2 * p + q}))
        wait_bytes(cam_sib.at[st, 1 - q], recv_sem.at[CA_SIB, st])
        cam_row[st, g] = cam_sib[st, 0] + cam_sib[st, 1]
        to_chips(lambda p: remote(cam_row.at[st, g], cam_row.at[st, g], CA_ROW, st, {"col": 2 * p + q}))

        for j in range(2):
            values = [pose[j, k] for k in range(8)]
            total = [-lane_sum(acc_pair[j, k]) for k in range(12)]
            turned, unit, length = rotation(values[0:4])
            scale = jnp.exp(values[7])
            h = [[scale * total[3 * k + n] for n in range(3)] for k in range(3)]
            grad_scale = sum(turned[k][n] * h[k][n] for k in range(3) for n in range(3))
            grads = rotation_grad(h, unit, length) + total[9:12] + [grad_scale]
            for k in range(8):
                pose[j, k], pose_m[j, k], pose_v[j, k] = adam_step(
                    values[k], grads[k], pose_m[j, k], pose_v[j, k], fix_one, fix_two, rates[2])

        wait_bytes(row_recv.at[st, pl.ds(0, CHIPS - 1)], recv_sem.at[GR_ALL, st])
        grad = row_recv[st, 0]
        for p in range(1, CHIPS):
            grad = grad + row_recv[st, p]

        wait_bytes(cam_row.at[st, pl.ds(0, CHIPS - 1)], recv_sem.at[CA_ROW, st])
        group = cam_row[st, 0]
        for p in range(1, CHIPS):
            group = group + cam_row[st, p]
        cam_all[st, r] = group
        to_rows(lambda p: remote(cam_all.at[st, r], cam_all.at[st, r], CA_ALL, st, {"row": p}))

        wait_bytes(col_recv.at[st, pl.ds(0, CHIPS - 1)], recv_sem.at[GC_ALL, st])
        col_owner[st, r] = col_recv[st, pl.ds(2 * r, 2)]
        to_rows(lambda p: remote(col_recv.at[st, pl.ds(2 * p, 2)], col_owner.at[st, r], GC_OWN, st, {"row": p}))

        wait_bytes(all_depth.at[st, pl.ds(0, ROWS - 1)], send_sem.at[OWN_COL])
        wait_bytes(row_depth.at[st, q, pl.ds(0, CHIPS - 1)], send_sem.at[ROW_ALL])
        wait_bytes(row_depth.at[st, q], send_sem.at[ROW_FWD])
        wait_bytes(col_depth.at[st, q, pl.ds(0, CHIPS - 1)], send_sem.at[COL_ALL])
        wait_bytes(col_depth.at[st, q, :, 1 - q], send_sem.at[COL_FWD])
        wait_bytes(row_sib.at[st], send_sem.at[GR_SIB])
        wait_bytes(row_recv.at[st, pl.ds(0, CHIPS - 1)], send_sem.at[GR_ALL])
        wait_bytes(col_grad.at[st, 1 - q, :, q], send_sem.at[GC_SIB])
        wait_bytes(cam_sib.at[st, q], send_sem.at[CA_SIB])
        wait_bytes(col_recv.at[st, pl.ds(0, CHIPS - 1)], send_sem.at[GC_ALL])
        wait_bytes(cam_row.at[st, pl.ds(0, CHIPS - 1)], send_sem.at[CA_ROW])

        wait_bytes(col_owner.at[st, pl.ds(0, ROWS - 1)], recv_sem.at[GC_OWN, st])
        pieces = []
        for x in range(2):
            for k in range(2):
                piece = col_owner[st, 0, x, k]
                for p in range(1, ROWS):
                    piece = piece + col_owner[st, p, x, k]
                pieces.append(piece)
        grad = grad + jnp.concatenate(pieces, axis=0)
        depth[...], depth_m[...], depth_v[...] = adam_step(
            depth[...], grad, depth_m[...], depth_v[...], fix_one, fix_two, rates[0])

        wait_bytes(cam_all.at[st, pl.ds(0, ROWS - 1)], send_sem.at[CA_ALL])
        wait_bytes(col_owner.at[st, pl.ds(0, ROWS - 1)], send_sem.at[GC_OWN])
        return carry

    lax.fori_loop(0, ADAM_STEPS, step, 0)

    last = ADAM_STEPS - 1
    depth_out[...] = depth[:, 0:HALF]
    small = lax.broadcasted_iota(jnp.int32, (8, 8), 1)
    for j in range(2):
        packed = jnp.zeros((8, 8), F32)
        for k in range(8):
            packed = jnp.where(small == k, pose[j, k][:, 0:8], packed)
        pair_out[:, j, :] = packed
    wait_bytes(cam_all.at[last, pl.ds(0, ROWS - 1)], recv_sem.at[CA_ALL, last])
    grad = cam_all[last, 0]
    for p in range(1, ROWS):
        grad = grad + cam_all[last, p]
    final, _, _ = adam_step(
        cam[...], grad, cam_m[...], cam_v[...], 1.0 - BETA_ONE**2, 1.0 - BETA_TWO**2, rates[1])
    camera_out[...] = final[:, 0:IMAGES]


def body(pointmaps, confidence, valid_blocks, log_depth, camera, pair_pose, step_sizes):
    vmem = pl.BlockSpec(memory_space=pltpu.VMEM)
    hbm = pl.BlockSpec(memory_space=pl.ANY)
    steps = ADAM_STEPS

    def f32(*shape):
        return pltpu.VMEM(shape, F32)

    kinds = 13
    maps = pointmaps.transpose(0, 1, 3, 2, 4)
    depth, cam, pair = pl.pallas_call(
        kernel,
        out_shape=(
            jax.ShapeDtypeStruct(log_depth.shape, F32),
            jax.ShapeDtypeStruct((8, IMAGES), F32),
            jax.ShapeDtypeStruct(pair_pose.shape, F32),
        ),
        in_specs=[hbm, hbm, vmem, vmem, vmem, vmem, pl.BlockSpec(memory_space=pltpu.SMEM)],
        out_specs=(vmem, vmem, vmem),
        scratch_shapes=[
            pltpu.VMEM(maps.shape, jnp.bfloat16),
            pltpu.VMEM(confidence.shape, jnp.bfloat16),
            f32(2 * 112 * 2 * 32, LANES),
            f32(TILES, 2, 8, LANES),
            f32(57, 8, LANES),
            f32(TILES, 7, 8, LANES),
            f32(2, 12, 8, LANES),
            f32(12, 8, LANES),
            f32(2, 12, 8, LANES),
            f32(8, WIDE), f32(8, WIDE), f32(8, WIDE),
            f32(2, 8, 8, LANES), f32(2, 8, 8, LANES), f32(2, 8, 8, LANES),
            f32(8, LANES), f32(8, LANES), f32(8, LANES),
            f32(steps, 2, CHIPS, 8, WIDE),
            f32(steps, ROWS, 2, 2, 2, WIDE),
            f32(steps, 2, CHIPS, 2, 2, WIDE),
            f32(2, CHIPS, 8, WIDE),
            f32(steps, CHIPS, 8, WIDE),
            f32(CHIPS, 8, WIDE),
            f32(steps, CHIPS, 8, WIDE),
            f32(steps, 2, CHIPS, 2, 2, WIDE),
            f32(steps, CHIPS, 2, 2, WIDE),
            f32(steps, ROWS, 2, 2, 2, WIDE),
            f32(steps, 2, 8, LANES),
            f32(steps, CHIPS, 8, LANES),
            f32(steps, ROWS, 8, LANES),
            pltpu.SemaphoreType.DMA((2,)),
            pltpu.SemaphoreType.DMA((kinds,)),
            pltpu.SemaphoreType.DMA((kinds, steps)),
        ],
        compiler_params=pltpu.CompilerParams(
            collective_id=0, has_side_effects=True, vmem_limit_bytes=56 * 1024 * 1024
        ),
        name="align",
    )(maps, confidence, valid_blocks, log_depth, camera.T, pair_pose, step_sizes)
    return depth, cam.T, pair


def solution(mesh):
    in_specs = (
        P("row", "col", None, None, None),
        P("row", "col", None, None),
        P("row", "col", None),
        P("row", "col"),
        P(),
        P("row", "col", None),
        P(),
    )
    out_specs = (P("row", "col"), P(), P("row", "col", None))
    return jax.shard_map(body, mesh=mesh, in_specs=in_specs, out_specs=out_specs, check_vma=False)
```

time: 826 us -> 85.6 us (0.10)
  waiting for transfers between devices: 447 us -> 0 us
  blocking collectives: 239 us -> 0 us
  other arithmetic: 82.2 us -> 0 us
  Pallas kernels: 0 us -> 80.7 us
  local copies, waits for them, and re-layouts: 33.6 us -> 3.89 us
  between operations: 17.1 us -> 0.64 us
    psum x4 -> x0, waiting for transfers between devices: 279 us -> none  [the longest x2 161 us: body(): col_total = lax.psum(col_grad, 'row')]
    unnamed x8 -> x0, waiting for transfers between devices: 167 us -> none
    psum x2 -> x0, blocking collectives: 164 us -> none  [body(): cam_total = lax.psum(cam_grad, ('row', 'col'))]
    pallas_call x0 -> x1, Pallas kernels: none -> 80.7 us  [body(): pl.pallas_call(kernel, out_shape=(jax.ShapeDtypeStruct(log_depth.shape, F...]
    all_gather x2 -> x0, blocking collectives: 75.8 us -> none  [body(): row_depth = lax.all_gather(depth_now, 'col', axis=1, tiled=True)]
    reduce_sum x14 -> x0, other arithmetic: 31.6 us -> none  [the longest x4 21 us: pair_loss(): pair_scale[..., None]]
    add_any x16 -> x0, other arithmetic: 21.7 us -> none  [the longest x8 20.3 us: pair_loss(): squared = squared + residual * residual]
    unnamed x80 -> x3, local copies, waits for them, and re-layouts: 16 us -> 3.89 us
  transfers between devices with their start and end apart: 6 -> 0, of which waited for: 6 -> 0; matrix products, arithmetic and copies ran while one was open for 6% -> 0% of each run, Pallas kernels for 0% -> 0%
where the time goes in v1:
time: 85.6 us; the launch traced here: 85.2 us
  Pallas kernels  80.7 us (94%)
  local copies, waits for them, and re-layouts  3.89 us (5%)
    pallas_call x1, Pallas kernels, body(): pl.pallas_call(kernel, out_shape=(jax.ShapeDtypeStruct(log_depth.shape, F...  80.7 us
    unnamed x3, local copies, waits for them, and re-layouts  3.89 us

profile of v1, /device:TPU:1, one launch (start us, length us, event | category | flops | bytes accessed | tf_op | source)
XLA Modules:
  0.0 85.2 jit_solution(17114982872811624821)
XLA Ops:
  0.6 80.7 %align.1 = (f32[8,448]{1,0:T(8,128)}, f32[8,64]{1,0:T(8,128)}, f32[8,2,8]{2,1,0:T(2,128)}) custom-call(bf16[8,2,3,2,14336]{4,3,2,1,0:T(2,128)(2,1)} %bitcast.3, bf16[8,2,2,14336]{3,2,1,0:T(2,128)(2,1)} %conf_hbm.1, s32[8,2,64]{2,1,0:T(2,128)} %valid_ref.1, f32[8,448]{1,0:T(8,128)} %depth_in.1, f32[8,64]{1,0:T(8,128)} %bitcast.4, f32[8,2,8]{2,1,0:T(2,128)} %pair_in.1, ...), custom_call_target="tpu_custom_call" | custom-call | tf_op jit(solution)/shard_map/align/pallas_call | solution.py:508
  81.3 1.3 %copy.13 = f32[8,448]{1,0:T(8,128)} copy(f32[8,448]{1,0:T(8,128)} %get-tuple-element.12) | data formatting | bytes 28672
  82.6 1.3 %copy.14 = f32[64,8]{0,1:T(8,128)} copy(f32[64,8]{0,1:T(8,128)} %bitcast.5) | data formatting | bytes 4096
  83.9 1.3 %copy.15 = f32[8,2,8]{2,1,0:T(2,128)} copy(f32[8,2,8]{2,1,0:T(2,128)} %get-tuple-element.14) | data formatting | bytes 1024

commit v2 on v0

v2 whole, which is shorter than its diff:
```python
import math

import jax
import jax.numpy as jnp
import numpy as np
from jax import lax
from jax.experimental import pallas as pl
from jax.experimental.pallas import tpu as pltpu
from jax.sharding import PartitionSpec as P

IMAGES = 64
IMG_WIDTH = 224
IMG_HEIGHT = 224
WIN_ROWS = 64
ADAM_STEPS = 2
BETA_ONE = 0.9
BETA_TWO = 0.999
ADAM_EPS = 0.001
SOFTEN = 0.01

ROWS = 8
COLS = 32
CHIPS = COLS // 2
SECONDS = 4
HALF = 448
WIDE = 512
TILES = 4
STRIP = 896
LANES = 128
MESH = pl.DeviceIdType.MESH
F32 = jnp.float32


def plain_rotation(w, x, y, z):
    length = jnp.sqrt(w * w + x * x + y * y + z * z)
    w, x, y, z = w / length, x / length, y / length, z / length
    return [
        [1.0 - 2.0 * (y * y + z * z), 2.0 * (x * y - w * z), 2.0 * (x * z + w * y)],
        [2.0 * (x * y + w * z), 1.0 - 2.0 * (x * x + z * z), 2.0 * (y * z - w * x)],
        [2.0 * (x * z - w * y), 2.0 * (y * z + w * x), 1.0 - 2.0 * (x * x + y * y)],
    ]


class Pair:
    def __init__(self, high, low):
        self.high = high
        self.low = low

    @staticmethod
    def of(value):
        return value if isinstance(value, Pair) else Pair(value, None)

    @staticmethod
    def closed(high, low):
        total = high + low
        return Pair(total, low - (total - high))

    @staticmethod
    def constant(value):
        high = float(np.float32(value))
        low = value - high
        return Pair(high, low if low else None)

    def __add__(self, other):
        other = Pair.of(other)
        total = self.high + other.high
        back = total - self.high
        rest = (self.high - (total - back)) + (other.high - back)
        for part in (self.low, other.low):
            rest = rest if part is None else rest + part
        return Pair.closed(total, rest)

    def __neg__(self):
        return Pair(-self.high, None if self.low is None else -self.low)

    def __sub__(self, other):
        return self + (-Pair.of(other))

    def twice(self):
        return Pair(2.0 * self.high, None if self.low is None else 2.0 * self.low)

    @staticmethod
    def split(value):
        wide = 4097.0 * value
        top = wide - (wide - value)
        return top, value - top

    def __mul__(self, other):
        other = Pair.of(other)
        product = self.high * other.high
        a, b = Pair.split(self.high)
        c, d = Pair.split(other.high)
        rest = ((a * c - product) + a * d + b * c) + b * d
        if self.low is not None:
            rest = rest + self.low * other.high
        if other.low is not None:
            rest = rest + self.high * other.low
        return Pair.closed(product, rest)

    def __truediv__(self, other):
        other = Pair.of(other)
        first = self.high / other.high
        rest = self - other * Pair(first, None)
        return Pair.closed(first, rest.high / other.high)

    def root(self):
        first = jnp.sqrt(self.high)
        rest = self - Pair(first, None) * Pair(first, None)
        return Pair.closed(first, rest.high / (2.0 * first))


def exact_exp(value):
    small = Pair(value * 0.0625, None)
    total = Pair.constant(1.0 / math.factorial(12))
    total = Pair(jnp.full_like(value, total.high), None)
    for k in range(11, -1, -1):
        total = total * small + Pair.constant(1.0 / math.factorial(k))
    for _ in range(4):
        total = total * total
    return total


def rotation(quaternion):
    w, x, y, z = [Pair.of(value) for value in quaternion]
    length = (w * w + x * x + y * y + z * z).root()
    w, x, y, z = w / length, x / length, y / length, z / length
    xx, yy, zz = x * x, y * y, z * z
    xy, xz, yz, wx, wy, wz = x * y, x * z, y * z, w * x, w * y, w * z
    one = Pair(1.0, None)
    turned = [
        [one - (yy + zz).twice(), (xy - wz).twice(), (xz + wy).twice()],
        [(xy + wz).twice(), one - (xx + zz).twice(), (yz - wx).twice()],
        [(xz - wy).twice(), (yz + wx).twice(), one - (xx + yy).twice()],
    ]
    return turned, (w, x, y, z), length


def rotation_grad(h, unit, length):
    w, x, y, z = unit
    sums = [h[0][1] + h[1][0], h[0][2] + h[2][0], h[1][2] + h[2][1]]
    turns = [h[2][1] - h[1][2], h[0][2] - h[2][0], h[1][0] - h[0][1]]
    dw = (z * turns[2] + y * turns[1] + x * turns[0]).twice()
    dx = (y * sums[0] + z * sums[1] + w * turns[0] - (x * (h[1][1] + h[2][2])).twice()).twice()
    dy = (x * sums[0] + z * sums[2] + w * turns[1] - (y * (h[0][0] + h[2][2])).twice()).twice()
    dz = (x * sums[1] + y * sums[2] + w * turns[2] - (z * (h[0][0] + h[1][1])).twice()).twice()
    along = w * dw + x * dx + y * dy + z * dz
    return [((part - axis * along) / length).high for part, axis in ((dw, w), (dx, x), (dy, y), (dz, z))]


def adam_step(param, grad, first, second, fix_one, fix_two, step_size):
    first = BETA_ONE * first + (1.0 - BETA_ONE) * grad
    second = BETA_TWO * second + (1.0 - BETA_TWO) * grad * grad
    update = step_size * (first / fix_one) / (jnp.sqrt(second / fix_two) + ADAM_EPS)
    return param - update, first, second


def lane_sum(value):
    return jnp.broadcast_to(jnp.sum(value, axis=1, keepdims=True), value.shape)


COL_DEPTH, ROW_DEPTH, ROW_GRAD, COL_GRAD, POSE, CAM_ROW, CAM_ALL, SWAP, FIRST_POSE, OWN_DEPTH = range(10)
KINDS = 10


def kernel(
    maps_hbm, conf_hbm, valid_ref, depth_in, camera_in, pair_in, rates,
    depth_out, camera_out, pair_out,
    raw, raw_conf, planes, outbox, uv, row_ray, col_ray, turn, tmp, acc_row, acc_col, sums,
    depth, depth_m, depth_v, first_pose, pose, pose_m, pose_v, cam, cam_m, cam_v,
    row_depth, all_depth, col_depth, row_grad, row_recv, col_grad, col_recv, cam_row, cam_all,
    load_sem, send_sem, recv_sem, all_sem,
):
    r = lax.axis_index("row")
    c = lax.axis_index("col")
    q = lax.rem(c, 2)
    g = lax.div(c, 2)
    z = lax.div(g, 2)
    x_lo = lax.rem(g, 2)
    inside = r == z
    sibling = (r, 2 * g + 1 - q)
    lane = lax.broadcasted_iota(jnp.int32, (8, LANES), 1)
    sub = lax.broadcasted_iota(jnp.int32, (8, LANES), 0)

    def chip_at(n):
        half = lax.div(n + 1, 2)
        return lax.rem(g + 8 + half * (1 - 2 * lax.rem(n, 2)), CHIPS)

    def remote(src, dst, kind, st, device):
        return pltpu.make_async_remote_copy(
            src_ref=src, dst_ref=dst, send_sem=send_sem.at[kind], recv_sem=recv_sem.at[kind, st],
            device_id=device, device_id_type=MESH,
        )

    def wait_bytes(ref, sem):
        pltpu.make_async_copy(ref, ref, sem).wait()

    def wait_slots(ref, sem):
        @pl.when(inside)
        def _():
            wait_bytes(ref.at[pl.ds(0, CHIPS - 1)], sem)

        @pl.when(jnp.logical_not(inside))
        def _():
            wait_bytes(ref, sem)

    def repeat(count, action):
        def one(n, carry):
            action(n)
            return carry
        lax.fori_loop(0, count, one, 0)

    load_maps = pltpu.make_async_copy(maps_hbm, raw, load_sem.at[0])
    load_conf = pltpu.make_async_copy(conf_hbm, raw_conf, load_sem.at[1])
    load_maps.start()
    load_conf.start()

    barrier = pltpu.get_barrier_semaphore()

    def greet(row, col):
        pl.semaphore_signal(barrier, inc=1, device_id=(row, col), device_id_type=MESH)

    def to_row_group(act):
        def one(n):
            p = chip_at(n)
            act(p, r, 2 * p + q)
        repeat(CHIPS - 1, one)

    def row_near(n):
        across = lax.div(n, 4)
        turn_y = lax.rem(n, 4)
        turn_y = turn_y + lax.div(turn_y, 2) - 2 * lax.div(turn_y, 3)
        return 4 * lax.rem(lax.div(r, 4) + across, 2) + lax.rem(lax.rem(r, 4) + turn_y, 4)

    def to_column(act):
        lax.fori_loop(1, ROWS, lambda n, carry: (act(row_near(ROWS - n)), carry)[1], 0)

    def to_column_chips(act):
        def one(n):
            act(lax.rem(r + lax.div(n, 2), ROWS), 2 * g + lax.rem(q + lax.rem(n, 2), 2))
        lax.fori_loop(1, 2 * ROWS, lambda n, carry: (one(n), carry)[1], 0)

    to_row_group(lambda p, row, col: greet(row, col))
    to_column(lambda row: greet(row, c))
    greet(*sibling)

    depth[...] = jnp.zeros_like(depth)
    depth[:, 0:HALF] = depth_in[...]
    depth[...] = pltpu.roll(depth[...], 64 * q, 1)
    for ref in (depth_m, depth_v, pose_m, pose_v, cam, cam_m, cam_v):
        ref[...] = jnp.zeros_like(ref)
    for j in range(2):
        loaded = pair_in[:, j, :]
        for k in range(8):
            first_pose[q, k, 8 * j : 8 * j + 8, :] = jnp.broadcast_to(loaded[:, k : k + 1], (8, LANES))
    cam[:, 0:IMAGES] = camera_in[...]
    for t in range(TILES):
        position = lane + (3 * q + t) * LANES
        downward = (
            (position >= IMG_WIDTH).astype(jnp.int32)
            + (position >= 2 * IMG_WIDTH).astype(jnp.int32)
            + (position >= 3 * IMG_WIDTH).astype(jnp.int32)
        )
        uv[t, 0] = (position - IMG_WIDTH * downward).astype(F32) - (IMG_WIDTH - 1) / 2.0
        uv[t, 1] = downward.astype(F32) + ((IMG_HEIGHT - WIN_ROWS) // 2 - (IMG_HEIGHT - 1) / 2.0)

    def prepare(m):
        lane64 = lax.broadcasted_iota(jnp.int32, (8, WIN_ROWS), 1)
        for away in (True, False):
            half = 1 - q if away else q
            for j in range(2):
                here = valid_ref[:, j, :].astype(F32)
                other = (ROWS * r + sub) != (2 * c + j)
                scale = jnp.where(other, 1.0 / (2.0 * (IMAGES - 1)), 0.0)
                line = [
                    scale * lane_sum_to(jnp.where(lane64 == 4 * m + 2 * half + a, here, 0.0)) for a in range(2)
                ]
                for t in range(TILES):
                    tile = 3 * half + t
                    start = pl.multiple_of(m * STRIP + tile * LANES, LANES)
                    put = outbox.at[m, j, t] if away else planes.at[q, m, j, t]
                    for i in range(8):
                        for k in range(3):
                            put[pl.ds(8 * k + i, 2, stride=32), :] = raw[i, j, k, :, pl.ds(start, LANES)].astype(F32)
                        put[pl.ds(24 + i, 2, stride=32), :] = raw_conf[i, j, :, pl.ds(start, LANES)].astype(F32)
                    position = lane + tile * LANES - HALF * half
                    keep = jnp.where(position < IMG_WIDTH, line[0], line[1])
                    keep = jnp.where((position >= 0) & (position < HALF), keep, 0.0)
                    for s in range(2):
                        put[32 * s + 24 : 32 * s + 32, :] = put[32 * s + 24 : 32 * s + 32, :] * keep

    def lane_sum_to(value):
        return jnp.broadcast_to(jnp.sum(value, axis=1, keepdims=True), (8, LANES))

    def swap_strip(m):
        remote(outbox.at[m], planes.at[q, m], SWAP, 0, sibling).start()

    load_maps.wait()
    load_conf.wait()
    repeat(CHIPS // 2, prepare)
    pl.semaphore_wait(barrier, CHIPS - 1 + ROWS - 1 + 1)

    lane16 = lax.broadcasted_iota(jnp.int32, (16, LANES), 1)
    sub16 = lax.broadcasted_iota(jnp.int32, (16, LANES), 0)
    image16 = jnp.where(sub16 < 8, 8 * r + sub16, SECONDS * g + lax.rem(sub16, SECONDS))

    def cameras():
        now = cam[...]
        return [
            lane_sum(jnp.where(lane16 == image16, jnp.broadcast_to(now[k : k + 1, :], (16, LANES)), 0.0))
            for k in range(8)
        ]

    def element(put, s, at, points, total):
        x = [put[32 * s + 8 * k : 32 * s + 8 * k + 8, :] for k in range(3)]
        weight = put[32 * s + 24 : 32 * s + 32, :]
        residual = [
            points[k] - (at[12] * (at[3 * k] * x[0] + at[3 * k + 1] * x[1] + at[3 * k + 2] * x[2]) + at[9 + k])
            for k in range(3)
        ]
        squared = SOFTEN + residual[0] * residual[0] + residual[1] * residual[1] + residual[2] * residual[2]
        pull = weight * lax.rsqrt(squared)
        grads = [pull * residual[k] for k in range(3)]
        sized = [at[12] * grads[k] for k in range(3)]
        terms = [sized[k] * x[n] for k in range(3) for n in range(3)] + grads
        total = terms if total is None else [a + b for a, b in zip(total, terms)]
        return grads, total

    def moments(grads, value, u, v, total):
        h = [grads[k] * value for k in range(3)]
        terms = [h[k] * u for k in range(3)] + [h[k] * v for k in range(3)] + h + list(grads)
        return terms if total is None else [a + b for a, b in zip(total, terms)]

    def rays(at, t, down, value):
        u = uv[t, 0]
        v = uv[t, 1] + down
        across = at(13 + t) * value
        below = v / at(12) * value
        z3 = [at(k) * across + at(3 + k) * below + at(6 + k) * value for k in range(3)]
        return u, v, z3, [z3[k] + at(9 + k) for k in range(3)]

    def pair_at(jj):
        rows = slice(8 * jj, 8 * jj + 8)
        return [turn[k, rows, :] for k in range(13)]

    def camera_grad(values, total):
        turned, unit, length = rotation(values[0:4])
        focal = exact_exp(values[7])
        h = [[Pair.of(total[k]) / focal, Pair.of(total[3 + k]) / focal, Pair.of(total[6 + k])] for k in range(3)]
        along = turned[0][0] * h[0][0] + turned[0][1] * h[0][1]
        for k in range(1, 3):
            along = along + turned[k][0] * h[k][0] + turned[k][1] * h[k][1]
        return rotation_grad(h, unit, length) + [total[9], total[10], total[11], -along.high]

    def add_slots(ref, count):
        total = ref[0]
        for p in range(1, count):
            total = total + ref[p]
        return total

    def step(st, carry):
        late = (st > 0).astype(F32)
        fix_one = (1.0 - BETA_ONE) + late * ((1.0 - BETA_ONE**2) - (1.0 - BETA_ONE))
        fix_two = (1.0 - BETA_TWO) + late * ((1.0 - BETA_TWO**2) - (1.0 - BETA_TWO))

        now = depth[...]
        for x in range(2):
            all_depth[st, r, x] = now[4 * x : 4 * x + 4, :]
        to_column(lambda row: pltpu.make_async_remote_copy(
            src_ref=all_depth.at[st, r], dst_ref=all_depth.at[st, r], send_sem=send_sem.at[OWN_DEPTH],
            recv_sem=all_sem.at[st, r], device_id=(row, c), device_id_type=MESH).start())
        row_depth[st, g] = now
        to_row_group(lambda p, row, col: remote(
            row_depth.at[st, g], row_depth.at[st, g], ROW_DEPTH, st, (row, col)).start())

        def pass_on(row):
            for x in range(2):
                p = 2 * row + x

                @pl.when(p != g)
                def _():
                    remote(all_depth.at[st, row, x], col_depth.at[st, g], COL_DEPTH, st, (r, 2 * p + q)).start()

        pass_on(r)

        @pl.when(st == 0)
        def _():
            remote(first_pose.at[q], first_pose.at[q], FIRST_POSE, 0, sibling).start()
            repeat(CHIPS // 2, swap_strip)

        sums[st, q] = jnp.zeros((12, 32, LANES), F32)
        acc_row[...] = jnp.zeros_like(acc_row)
        acc_col[...] = jnp.zeros_like(acc_col)

        def arrive(n, carry):
            row = row_near(n)
            wait_bytes(all_depth.at[st, row], all_sem.at[st, row])
            pass_on(row)
            return carry

        lax.fori_loop(1, ROWS, arrive, 0)
        col_depth[st, g] = all_depth[st, z, x_lo]

        @pl.when(st == 0)
        def _():
            def rest(n):
                prepare(CHIPS // 2 + n)
                swap_strip(CHIPS // 2 + n)
            repeat(CHIPS // 2, rest)
            wait_bytes(first_pose.at[1 - q], recv_sem.at[FIRST_POSE, 0])
            for k in range(8):
                pose[k, 0:16, :] = first_pose[0, k]
                pose[k, 16:32, :] = first_pose[1, k]

        @pl.when(st > 0)
        def _():
            wait_bytes(cam_all.at[st - 1, pl.ds(0, 2 * ROWS - 1)], recv_sem.at[CAM_ALL, st - 1])
            cam[...], cam_m[...], cam_v[...] = adam_step(
                cam[...], add_slots(cam_all.at[st - 1], 2 * ROWS), cam_m[...], cam_v[...],
                1.0 - BETA_ONE, 1.0 - BETA_TWO, rates[1])

        values = cameras()
        turned = plain_rotation(*values[0:4])
        focal = jnp.exp(values[7])

        def keep_ray(ref, at, rows):
            for k in range(3):
                for n in range(3):
                    ref[at + (3 * n + k,)] = jnp.broadcast_to(turned[k][n][rows], (8, LANES))
                ref[at + (9 + k,)] = jnp.broadcast_to(values[4 + k][rows], (8, LANES))
            ref[at + (12,)] = jnp.broadcast_to(focal[rows], (8, LANES))
            for t in range(TILES):
                ref[at + (13 + t,)] = uv[t, 0] / ref[at + (12,)]

        keep_ray(row_ray, (), slice(0, 8))
        for jj in range(SECONDS):
            keep_ray(col_ray, (jj,), slice(8 + jj, 9 + jj))
        values = [pose[k] for k in range(8)]
        turned = plain_rotation(*values[0:4])
        for k in range(3):
            for n in range(3):
                turn[3 * k + n] = turned[k][n]
            turn[9 + k] = values[4 + k]
        turn[12] = jnp.exp(values[7])

        @pl.when(st == 0)
        def _():
            wait_bytes(planes.at[1 - q], recv_sem.at[SWAP, 0])

        wait_bytes(row_depth.at[st, pl.ds(0, CHIPS - 1)], recv_sem.at[ROW_DEPTH, st])

        def side_rows(n):
            m = chip_at(n)
            down = (4 * m).astype(F32)
            for t in range(TILES):
                value = jnp.exp(row_depth[st, m, :, t * LANES : (t + 1) * LANES])
                _, _, z3, points = rays(lambda k: row_ray[k], t, down, value)
                tmp[t, 6] = value
                for k in range(3):
                    tmp[t, k] = z3[k]
                    tmp[t, 7 + k] = points[k]
            for jj in range(SECONDS):
                at = pair_at(jj)
                total = None
                for t in range(TILES):
                    points = [tmp[t, 7 + k] for k in range(3)]
                    grads, total = element(planes.at[jj // 2, m, jj % 2, t], 0, at, points, total)
                    for k in range(3):
                        tmp[t, 3 + k] = grads[k] if jj == 0 else tmp[t, 3 + k] + grads[k]
                for k in range(12):
                    sums[st, q, k, 8 * jj : 8 * jj + 8, :] += total[k]
            total = None
            for t in range(TILES):
                grads = [tmp[t, 3 + k] for k in range(3)]
                z3 = [tmp[t, k] for k in range(3)]
                row_grad[m, :, t * LANES : (t + 1) * LANES] = (
                    grads[0] * z3[0] + grads[1] * z3[1] + grads[2] * z3[2])
                total = moments(grads, tmp[t, 6], uv[t, 0], uv[t, 1] + down, total)
            for k in range(12):
                acc_row[k] += total[k]

            @pl.when(n < CHIPS - 1)
            def _():
                remote(row_grad.at[m], row_recv.at[st, g], ROW_GRAD, st, (r, 2 * m + q)).start()

        repeat(CHIPS, side_rows)
        row_recv[st, g] = row_grad[g]
        wait_bytes(col_depth.at[st, pl.ds(0, CHIPS - 1)], recv_sem.at[COL_DEPTH, st])

        def side_cols(n):
            m = chip_at(n)
            down = (4 * m).astype(F32)
            values = jnp.exp(col_depth[st, m])
            for jj in range(SECONDS):
                at = pair_at(jj)
                total = None
                cam_total = None
                for t in range(TILES):
                    value = jnp.broadcast_to(values[jj : jj + 1, t * LANES : (t + 1) * LANES], (8, LANES))
                    u, v, z3, points = rays(lambda k: col_ray[jj, k], t, down, value)
                    grads, total = element(planes.at[jj // 2, m, jj % 2, t], 1, at, points, total)
                    mine = grads[0] * z3[0] + grads[1] * z3[1] + grads[2] * z3[2]
                    col_grad[m, jj : jj + 1, t * LANES : (t + 1) * LANES] = jnp.sum(mine, axis=0, keepdims=True)
                    cam_total = moments(grads, value, u, v, cam_total)
                for k in range(12):
                    sums[st, q, k, 8 * jj : 8 * jj + 8, :] += total[k]
                for k in range(12):
                    acc_col[k, jj] += cam_total[k]

            @pl.when(jnp.logical_not(inside & (m == g)))
            def _():
                remote(col_grad.at[m], col_recv.at[st, 2 * r + x_lo], COL_GRAD, st, (z, 2 * m + q)).start()

        repeat(CHIPS, side_cols)

        @pl.when(inside)
        def _():
            col_recv[st, 2 * r + x_lo] = col_grad[g]

        total = []
        for k in range(12):
            rows = [acc_row[k]] + [jnp.sum(acc_col[k, jj], axis=0, keepdims=True) for jj in range(SECONDS)]
            total.append(lane_sum(jnp.concatenate(rows + [jnp.zeros((4, LANES), F32)], axis=0)))
        part = camera_grad(cameras(), total)
        counted = (lane16 == image16) & (sub16 < 8 + SECONDS)
        cam_row[st, g] = jnp.concatenate(
            [jnp.sum(jnp.where(counted, part[k], 0.0), axis=0, keepdims=True) for k in range(8)], axis=0)
        to_row_group(lambda p, row, col: remote(
            cam_row.at[st, g], cam_row.at[st, g], CAM_ROW, st, (row, col)).start())
        remote(sums.at[st, q], sums.at[st, q], POSE, st, sibling).start()

        wait_bytes(all_depth.at[st, pl.ds(0, ROWS - 1)], send_sem.at[OWN_DEPTH])
        wait_bytes(col_depth.at[st, pl.ds(0, CHIPS - 1)], send_sem.at[COL_DEPTH])
        wait_bytes(row_depth.at[st, pl.ds(0, CHIPS - 1)], send_sem.at[ROW_DEPTH])

        wait_bytes(sums.at[st, 1 - q], recv_sem.at[POSE, st])
        values = [pose[k] for k in range(8)]
        total = [-lane_sum(sums[st, 0, k] + sums[st, 1, k]) for k in range(12)]
        turned, pull_back = jax.vjp(plain_rotation, *values[0:4])
        h = [[total[3 * k + n] for n in range(3)] for k in range(3)]
        grad_scale = sum(turned[k][n] * h[k][n] for k in range(3) for n in range(3))
        grads = list(pull_back(h)) + total[9:12] + [grad_scale]
        for k in range(8):
            pose[k], pose_m[k], pose_v[k] = adam_step(
                values[k], grads[k], pose_m[k], pose_v[k], fix_one, fix_two, rates[2])

        wait_bytes(cam_row.at[st, pl.ds(0, CHIPS - 1)], recv_sem.at[CAM_ROW, st])
        cam_all[st, 2 * r + q] = add_slots(cam_row.at[st], CHIPS)
        to_column_chips(lambda row, col: remote(
            cam_all.at[st, 2 * r + q], cam_all.at[st, 2 * r + q], CAM_ALL, st, (row, col)).start())

        wait_bytes(sums.at[st, q], send_sem.at[POSE])
        wait_bytes(row_recv.at[st, pl.ds(0, CHIPS - 1)], recv_sem.at[ROW_GRAD, st])
        grad = add_slots(row_recv.at[st], CHIPS)
        wait_bytes(row_recv.at[st, pl.ds(0, CHIPS - 1)], send_sem.at[ROW_GRAD])
        wait_bytes(cam_row.at[st, pl.ds(0, CHIPS - 1)], send_sem.at[CAM_ROW])
        wait_slots(col_recv.at[st], recv_sem.at[COL_GRAD, st])
        pieces = []
        for x in range(2):
            piece = col_recv[st, x]
            for p in range(1, ROWS):
                piece = piece + col_recv[st, 2 * p + x]
            pieces.append(piece)
        grad = grad + jnp.concatenate(pieces, axis=0)
        depth[...], depth_m[...], depth_v[...] = adam_step(
            depth[...], grad, depth_m[...], depth_v[...], fix_one, fix_two, rates[0])
        wait_slots(col_recv.at[st], send_sem.at[COL_GRAD])
        wait_bytes(cam_all.at[st, pl.ds(0, 2 * ROWS - 1)], send_sem.at[CAM_ALL])
        return carry

    lax.fori_loop(0, ADAM_STEPS, step, 0)

    last = ADAM_STEPS - 1
    wait_bytes(outbox, send_sem.at[SWAP])
    wait_bytes(first_pose.at[q], send_sem.at[FIRST_POSE])
    depth_out[...] = pltpu.roll(depth[...], (WIDE - 64 * q) % WIDE, 1)[:, 0:HALF]
    small = lax.broadcasted_iota(jnp.int32, (8, 8), 1)
    for j in range(2):
        packed = jnp.zeros((8, 8), F32)
        for k in range(8):
            mine = pose[k, pl.ds(pl.multiple_of(16 * q + 8 * j, 8), 8), :]
            packed = jnp.where(small == k, mine[:, 0:8], packed)
        pair_out[:, j, :] = packed
    wait_bytes(cam_all.at[last, pl.ds(0, 2 * ROWS - 1)], recv_sem.at[CAM_ALL, last])
    final, _, _ = adam_step(
        cam[...], add_slots(cam_all.at[last], 2 * ROWS), cam_m[...], cam_v[...],
        1.0 - BETA_ONE**2, 1.0 - BETA_TWO**2, rates[1])
    camera_out[...] = final[:, 0:IMAGES]


def body(pointmaps, confidence, valid_blocks, log_depth, camera, pair_pose, step_sizes):
    vmem = pl.BlockSpec(memory_space=pltpu.VMEM)
    hbm = pl.BlockSpec(memory_space=pl.ANY)
    steps = ADAM_STEPS
    maps = pointmaps.transpose(0, 1, 3, 2, 4)

    def f32(*shape):
        return pltpu.VMEM(shape, F32)

    depth, cam, pair = pl.pallas_call(
        kernel,
        out_shape=(
            jax.ShapeDtypeStruct(log_depth.shape, F32),
            jax.ShapeDtypeStruct((8, IMAGES), F32),
            jax.ShapeDtypeStruct(pair_pose.shape, F32),
        ),
        in_specs=[hbm, hbm, vmem, vmem, vmem, vmem, pl.BlockSpec(memory_space=pltpu.SMEM)],
        out_specs=(vmem, vmem, vmem),
        scratch_shapes=[
            pltpu.VMEM(maps.shape, jnp.bfloat16),
            pltpu.VMEM(confidence.shape, jnp.bfloat16),
            f32(2, CHIPS, 2, TILES, 64, LANES),
            f32(CHIPS, 2, TILES, 64, LANES),
            f32(TILES, 2, 8, LANES),
            f32(17, 8, LANES),
            f32(SECONDS, 17, 8, LANES),
            f32(13, 32, LANES),
            f32(TILES, 10, 8, LANES),
            f32(12, 8, LANES),
            f32(12, SECONDS, 8, LANES),
            f32(steps, 2, 12, 32, LANES),
            f32(8, WIDE), f32(8, WIDE), f32(8, WIDE),
            f32(2, 8, 16, LANES),
            f32(8, 32, LANES), f32(8, 32, LANES), f32(8, 32, LANES),
            f32(8, LANES), f32(8, LANES), f32(8, LANES),
            f32(steps, CHIPS, 8, WIDE),
            f32(steps, ROWS, 2, 4, WIDE),
            f32(steps, CHIPS, 4, WIDE),
            f32(CHIPS, 8, WIDE),
            f32(steps, CHIPS, 8, WIDE),
            f32(CHIPS, 4, WIDE),
            f32(steps, CHIPS, 4, WIDE),
            f32(steps, CHIPS, 8, LANES),
            f32(steps, 2 * ROWS, 8, LANES),
            pltpu.SemaphoreType.DMA((2,)),
            pltpu.SemaphoreType.DMA((KINDS,)),
            pltpu.SemaphoreType.DMA((KINDS, steps)),
            pltpu.SemaphoreType.DMA((steps, ROWS)),
        ],
        compiler_params=pltpu.CompilerParams(
            collective_id=0, has_side_effects=True, vmem_limit_bytes=56 * 1024 * 1024
        ),
        name="align",
    )(maps, confidence, valid_blocks, log_depth, camera.T, pair_pose, step_sizes)
    return depth, cam.T, pair


def solution(mesh):
    in_specs = (
        P("row", "col", None, None, None),
        P("row", "col", None, None),
        P("row", "col", None),
        P("row", "col"),
        P(),
        P("row", "col", None),
        P(),
    )
    out_specs = (P("row", "col"), P(), P("row", "col", None))
    return jax.shard_map(body, mesh=mesh, in_specs=in_specs, out_specs=out_specs, check_vma=False)
```

time: 826 us -> 71.7 us (0.09)
  waiting for transfers between devices: 447 us -> 0 us
  blocking collectives: 239 us -> 0 us
  other arithmetic: 82.2 us -> 0 us
  Pallas kernels: 0 us -> 66.8 us
  local copies, waits for them, and re-layouts: 33.6 us -> 3.89 us
  between operations: 17.1 us -> 0.64 us
    psum x4 -> x0, waiting for transfers between devices: 279 us -> none  [the longest x2 161 us: body(): col_total = lax.psum(col_grad, 'row')]
    unnamed x8 -> x0, waiting for transfers between devices: 167 us -> none
    psum x2 -> x0, blocking collectives: 164 us -> none  [body(): cam_total = lax.psum(cam_grad, ('row', 'col'))]
    all_gather x2 -> x0, blocking collectives: 75.8 us -> none  [body(): row_depth = lax.all_gather(depth_now, 'col', axis=1, tiled=True)]
    pallas_call x0 -> x1, Pallas kernels: none -> 66.8 us  [body(): pl.pallas_call(kernel, out_shape=(jax.ShapeDtypeStruct(log_depth.shape, F...]
    reduce_sum x14 -> x0, other arithmetic: 31.6 us -> none  [the longest x4 21 us: pair_loss(): pair_scale[..., None]]
    add_any x16 -> x0, other arithmetic: 21.7 us -> none  [the longest x8 20.3 us: pair_loss(): squared = squared + residual * residual]
    unnamed x80 -> x3, local copies, waits for them, and re-layouts: 16 us -> 3.89 us
  transfers between devices with their start and end apart: 6 -> 0, of which waited for: 6 -> 0; matrix products, arithmetic and copies ran while one was open for 6% -> 0% of each run, Pallas kernels for 0% -> 0%
where the time goes in v2:
time: 71.7 us; the launch traced here: 71.3 us
  Pallas kernels  66.8 us (93%)
  local copies, waits for them, and re-layouts  3.89 us (5%)
    pallas_call x1, Pallas kernels, body(): pl.pallas_call(kernel, out_shape=(jax.ShapeDtypeStruct(log_depth.shape, F...  66.8 us
    unnamed x3, local copies, waits for them, and re-layouts  3.89 us

profile of v2, /device:TPU:1, one launch (start us, length us, event | category | flops | bytes accessed | tf_op | source)
XLA Modules:
  0.0 71.3 jit_solution(3264187309804784039)
XLA Ops:
  0.6 66.8 %align.1 = (f32[8,448]{1,0:T(8,128)}, f32[8,64]{1,0:T(8,128)}, f32[8,2,8]{2,1,0:T(2,128)}) custom-call(bf16[8,2,3,2,14336]{4,3,2,1,0:T(2,128)(2,1)} %bitcast.3, bf16[8,2,2,14336]{3,2,1,0:T(2,128)(2,1)} %conf_hbm.1, s32[8,2,64]{2,1,0:T(2,128)} %valid_ref.1, f32[8,448]{1,0:T(8,128)} %depth_in.1, f32[8,64]{1,0:T(8,128)} %bitcast.4, f32[8,2,8]{2,1,0:T(2,128)} %pair_in.1, ...), custom_call_target="tpu_custom_call" | custom-call | tf_op jit(solution)/shard_map/align/pallas_call | solution.py:599
  67.4 1.3 %copy.13 = f32[8,448]{1,0:T(8,128)} copy(f32[8,448]{1,0:T(8,128)} %get-tuple-element.12) | data formatting | bytes 28672
  68.7 1.3 %copy.14 = f32[64,8]{0,1:T(8,128)} copy(f32[64,8]{0,1:T(8,128)} %bitcast.5) | data formatting | bytes 4096
  70.0 1.3 %copy.15 = f32[8,2,8]{2,1,0:T(2,128)} copy(f32[8,2,8]{2,1,0:T(2,128)} %get-tuple-element.14) | data formatting | bytes 1024

commit v3 on v2

--- a/solution.py
+++ b/solution.py
@@ -164,7 +164,7 @@
 
 def kernel(
     maps_hbm, conf_hbm, valid_ref, depth_in, camera_in, pair_in, rates,
-    depth_out, camera_out, pair_out,
+    packed_out,
     raw, raw_conf, planes, outbox, uv, row_ray, col_ray, turn, tmp, acc_row, acc_col, sums,
     depth, depth_m, depth_v, first_pose, pose, pose_m, pose_v, cam, cam_m, cam_v,
     row_depth, all_depth, col_depth, row_grad, row_recv, col_grad, col_recv, cam_row, cam_all,
@@ -572,19 +572,26 @@
     last = ADAM_STEPS - 1
     wait_bytes(outbox, send_sem.at[SWAP])
     wait_bytes(first_pose.at[q], send_sem.at[FIRST_POSE])
-    depth_out[...] = pltpu.roll(depth[...], (WIDE - 64 * q) % WIDE, 1)[:, 0:HALF]
-    small = lax.broadcasted_iota(jnp.int32, (8, 8), 1)
+    packed_out[:, 0:WIDE] = pltpu.roll(depth[...], (WIDE - 64 * q) % WIDE, 1)
+    poses = jnp.zeros((8, LANES), F32)
     for j in range(2):
-        packed = jnp.zeros((8, 8), F32)
         for k in range(8):
             mine = pose[k, pl.ds(pl.multiple_of(16 * q + 8 * j, 8), 8), :]
-            packed = jnp.where(small == k, mine[:, 0:8], packed)
-        pair_out[:, j, :] = packed
+            poses = jnp.where(lane == 8 * j + k, mine, poses)
+    packed_out[:, WIDE + LANES : WIDE + 2 * LANES] = poses
     wait_bytes(cam_all.at[last, pl.ds(0, 2 * ROWS - 1)], recv_sem.at[CAM_ALL, last])
     final, _, _ = adam_step(
         cam[...], add_slots(cam_all.at[last], 2 * ROWS), cam_m[...], cam_v[...],
         1.0 - BETA_ONE**2, 1.0 - BETA_TWO**2, rates[1])
-    camera_out[...] = final[:, 0:IMAGES]
+    packed_out[:, WIDE : WIDE + LANES] = final
+
+
+def unpack(packed, depth_out, camera_out, pair_out):
+    depth_out[...] = packed[:, 0:HALF]
+    camera_out[...] = packed[:, WIDE : WIDE + IMAGES]
+    poses = packed[:, WIDE + LANES : WIDE + 2 * LANES]
+    pair_out[:, 0, :] = poses[:, 0:8]
+    pair_out[:, 1, :] = poses[:, 8:16]
 
 
 def body(pointmaps, confidence, valid_blocks, log_depth, camera, pair_pose, step_sizes):
@@ -596,15 +603,11 @@
     def f32(*shape):
         return pltpu.VMEM(shape, F32)
 
-    depth, cam, pair = pl.pallas_call(
+    packed = pl.pallas_call(
         kernel,
-        out_shape=(
-            jax.ShapeDtypeStruct(log_depth.shape, F32),
-            jax.ShapeDtypeStruct((8, IMAGES), F32),
-            jax.ShapeDtypeStruct(pair_pose.shape, F32),
-        ),
+        out_shape=jax.ShapeDtypeStruct((8, WIDE + 2 * LANES), F32),
         in_specs=[hbm, hbm, vmem, vmem, vmem, vmem, pl.BlockSpec(memory_space=pltpu.SMEM)],
-        out_specs=(vmem, vmem, vmem),
+        out_specs=vmem,
         scratch_shapes=[
             pltpu.VMEM(maps.shape, jnp.bfloat16),
             pltpu.VMEM(confidence.shape, jnp.bfloat16),
@@ -641,6 +644,17 @@
         ),
         name="align",
     )(maps, confidence, valid_blocks, log_depth, camera.T, pair_pose, step_sizes)
+    depth, cam, pair = pl.pallas_call(
+        unpack,
+        out_shape=(
+            jax.ShapeDtypeStruct(log_depth.shape, F32),
+            jax.ShapeDtypeStruct((8, IMAGES), F32),
+            jax.ShapeDtypeStruct(pair_pose.shape, F32),
+        ),
+        in_specs=[vmem],
+        out_specs=(vmem, vmem, vmem),
+        name="unpack",
+    )(packed)
     return depth, cam.T, pair
 
 

time: 71.7 us -> 69.1 us (0.964)
  local copies, waits for them, and re-layouts: 3.89 us -> 0 us
  Pallas kernels: 66.8 us -> 68.2 us
    unnamed x3 -> x0, local copies, waits for them, and re-layouts: 3.89 us -> none
    pallas_call x1 -> x2, Pallas kernels: 66.8 us -> 68.2 us  [the longest x1 66.8 us: body(): pl.pallas_call(kernel, out_shape=jax.ShapeDtypeStruct((8, WIDE + 2 * LANE...]
where the time goes in v3:
time: 69.1 us; the launch traced here: 68.9 us
  Pallas kernels  68.2 us (99%)
    pallas_call x1, Pallas kernels, body(): pl.pallas_call(kernel, out_shape=jax.ShapeDtypeStruct((8, WIDE + 2 * LANE...  66.8 us
    pallas_call x1, Pallas kernels, body(): pl.pallas_call(unpack, out_shape=(jax.ShapeDtypeStruct(log_depth.shape, F...  1.42 us

profile of v3, /device:TPU:1, one launch (start us, length us, event | category | flops | bytes accessed | tf_op | source)
XLA Modules:
  0.0 68.9 jit_solution(7685765080764377379)
XLA Ops:
  0.6 66.8 %align.1.packed = f32[8,768]{1,0:T(8,128)} custom-call(bf16[8,2,3,2,14336]{4,3,2,1,0:T(2,128)(2,1)} %bitcast.3, bf16[8,2,2,14336]{3,2,1,0:T(2,128)(2,1)} %conf_hbm.1, s32[8,2,64]{2,1,0:T(2,128)} %valid_ref.1, f32[8,448]{1,0:T(8,128)} %depth_in.1, f32[8,64]{1,0:T(8,128)} %bitcast.4, f32[8,2,8]{2,1,0:T(2,128)} %pair_in.1, f32[3]{0:T(128)} %rates.1), custom_call_target="tpu_custom_call" | custom-call | tf_op jit(solution)/shard_map/align/pallas_call | solution.py:606
  67.5 1.4 %unpack.1 = (f32[8,448]{1,0:T(8,128)}, f32[8,64]{1,0:T(8,128)}, f32[8,2,8]{2,1,0:T(2,128)}) custom-call(f32[8,768]{1,0:T(8,128)} %align.1.packed), custom_call_target="tpu_custom_call" | custom-call | tf_op jit(solution)/shard_map/unpack/pallas_call | solution.py:647
